TPU v7x, 32 devices: a whole 2x2x4 slice. The times are simulated.
32 devices in a mesh: groups: 2 (over y), pr: 4 (over z), pc: 4 (over x, core).
Axes of the slice: x: 2, y: 2, z: 4, core: 2. Of those that a mesh axis runs over, the one named last changes fastest.
Arguments:
- matrix: float32 [2, 2048, 1, 2048], P('groups', 'pr', None, 'pc'), parts along dimension 0, as said below
Outputs:
- factored: float32 [2, 2048, 1, 2048], P('groups', 'pr', None, 'pc'), parts along dimension 0
There are 2 independent parts, one for each index of `groups`. A program takes and returns all parts, laid end to end along the dimension named above; each array names one. Nothing has to cross between parts.
Inputs may be any that keep to these rules, and one draw needn't show every extreme that they name: The symmetric matrix given by the lower triangle of matrix is positive definite.
All inputs are finite; a program needn't handle non-finite values.
Results may differ from a plain program's by a relative error of at most 0.0001.
Values sent between devices are 32-bit elements; how exact they have to be, the bound alone decides.
A program may use at most 64 MiB of HBM per device.

v0:
```python
from functools import partial

import jax
import jax.numpy as jnp
from jax import lax
from jax.sharding import PartitionSpec as P


def from_root(shard, axis, root):
    mine = lax.axis_index(axis) == root
    return lax.psum(jnp.where(mine, shard, jnp.zeros_like(shard)), axis)


def symmetric(block):
    return jnp.tril(block) + jnp.tril(block, -1).T


def right_solve(factor, block):
    return lax.linalg.triangular_solve(factor, block, left_side=False, lower=True, transpose_a=True)


def factor_panel(tiles, step):
    row_count = tiles.shape[0]
    col_count = tiles.shape[2]
    rows_axis = lax.axis_size("pr")
    cols_axis = lax.axis_size("pc")
    my_row = lax.axis_index("pr")
    my_col = lax.axis_index("pc")
    diag_a = step // rows_axis
    diag_r = step % rows_axis
    diag_b = step // cols_axis
    diag_c = step % cols_axis
    solver = None
    column_list = []
    diagonal = from_root(tiles[diag_a, :, diag_b, :], "pr", diag_r)
    factor = jnp.linalg.cholesky(symmetric(diagonal))
    solver = jax.vmap(partial(right_solve, factor))
    owned = solver(tiles[:, :, diag_b, :])
    panel_rows = from_root(owned, "pc", diag_c)
    for index in range(col_count):
        global_col = index * cols_axis + my_col
        piece = lax.dynamic_index_in_dim(panel_rows, global_col // rows_axis, 0, keepdims=False)
        column_list.append(from_root(piece, "pr", global_col % rows_axis))
    panel_cols = jnp.stack(column_list)
    global_row = jnp.arange(row_count, dtype=jnp.int32) * rows_axis + my_row
    former = tiles[:, :, diag_b, :]
    written = jnp.where(
        (global_row > step)[:, None, None],
        panel_rows,
        jnp.where((global_row == step)[:, None, None], factor[None], former),
    )
    column = jnp.where(my_col == diag_c, written, former)
    tiles = tiles.at[:, :, diag_b, :].set(column)
    return (tiles, panel_rows, panel_cols)


def update(tiles, panel_rows, panel_cols, step, col_list):
    row_count = tiles.shape[0]
    rows_axis = lax.axis_size("pr")
    cols_axis = lax.axis_size("pc")
    my_row = lax.axis_index("pr")
    my_col = lax.axis_index("pc")
    global_row = jnp.arange(row_count, dtype=jnp.int32) * rows_axis + my_row
    for index in col_list:
        global_col = index * cols_axis + my_col
        product = jnp.einsum(
            "apq,sq->aps",
            panel_rows,
            panel_cols[index],
            precision=lax.Precision.HIGHEST,
            preferred_element_type=jnp.float32,
        )
        keep = (global_row > step) & (global_col > step) & (global_row >= global_col)
        current = tiles[:, :, index, :]
        tiles = tiles.at[:, :, index, :].set(
            jnp.where(keep[:, None, None], current - product, current)
        )
    return tiles


def on_device(matrix):
    tiles = matrix
    col_count = tiles.shape[2]
    tiles, first_rows, first_cols = factor_panel(tiles, 0)
    tiles = update(tiles, first_rows, first_cols, 0, list(range(col_count)))
    tiles, second_rows, second_cols = factor_panel(tiles, 1)
    tiles = update(tiles, second_rows, second_cols, 1, list(range(col_count)))
    return tiles


def solution(mesh):
    in_specs = (P("groups", "pr", None, "pc"),)
    out_specs = P("groups", "pr", None, "pc")
    return jax.shard_map(
        on_device, mesh=mesh, in_specs=in_specs, out_specs=out_specs, check_vma=False
    )
```

profile of v0, /device:TPU:0, one launch (start us, length us, event | category | flops | bytes accessed | tf_op | source)
XLA Modules:
  0.0 612.4 jit_solution(12072118578654381595)
XLA Ops:
  10.1 54.6 %all-reduce.8.cloned.1.call-done = f32[512,512]{0,1:T(8,128)} async-done(((f32[512,512]{0,1:T(8,128)}), f32[512,512]{0,1:T(8,128)}) %all-reduce.8.cloned.1.call-update) | async-done | bytes 1048592 | tf_op jit(solution)/shard_map/psum | solution.py:11
  70.4 11.7 %cholesky.286 = f32[128,128]{1,0:T(8,128)S(1)} custom-call(f32[128,128]{1,0:T(8,128)S(1)} %copy.7), custom_call_target="Cholesky" | custom-call | tf_op jit(solution)/shard_map/jit(cholesky)/cholesky | solution.py:36
  82.2 9.8 %custom-call.27 = f32[1,128,128]{1,2,0:T(8,128)S(1)} custom-call(f32[1,128,128]{2,1,0:T(8,128)S(1)} %get-tuple-element.112), custom_call_target="InvertDiagBlocksLowerTriangular" | custom-call | tf_op jit(solution)/shard_map/jit(cholesky)/cholesky | solution.py:36
  95.0 11.7 %cholesky.305 = f32[128,128]{1,0:T(8,128)S(1)} custom-call(f32[128,128]{1,0:T(8,128)S(1)} %copy.9), custom_call_target="Cholesky" | custom-call | tf_op jit(solution)/shard_map/jit(cholesky)/cholesky | solution.py:36
  106.9 10.0 %custom-call.28 = f32[1,128,128]{1,2,0:T(8,128)S(1)} custom-call(f32[1,128,128]{2,1,0:T(8,128)S(1)} %get-tuple-element.110), custom_call_target="InvertDiagBlocksLowerTriangular" | custom-call | tf_op jit(solution)/shard_map/jit(cholesky)/cholesky | solution.py:36
  118.8 11.7 %cholesky.326 = f32[128,128]{1,0:T(8,128)S(1)} custom-call(f32[128,128]{1,0:T(8,128)S(1)} %copy.15), custom_call_target="Cholesky" | custom-call | tf_op jit(solution)/shard_map/jit(cholesky)/cholesky | solution.py:36
  130.7 9.8 %custom-call.29 = f32[1,128,128]{1,2,0:T(8,128)S(1)} custom-call(f32[1,128,128]{2,1,0:T(8,128)S(1)} %get-tuple-element.108), custom_call_target="InvertDiagBlocksLowerTriangular" | custom-call | tf_op jit(solution)/shard_map/jit(cholesky)/cholesky | solution.py:36
  142.2 12.1 %cholesky.343 = f32[128,128]{1,0:T(8,128)S(1)} custom-call(f32[128,128]{1,0:T(8,128)S(1)} %copy.19), custom_call_target="Cholesky" | custom-call | tf_op jit(solution)/shard_map/jit(cholesky)/cholesky | solution.py:36
  159.2 8.9 %while.8 = (s32[]{:T(128)}, f32[512,512]{0,1:T(8,128)S(1)}, s32[4,2]{0,1:T(2,128)S(1)}, f32[4,128,128]{2,1,0:T(8,128)S(1)}, s32[]{:T(128)}) while((s32[]{:T(128)}, f32[512,512]{0,1:T(8,128)S(1)}, s32[4,2]{0,1:T(2,128)S(1)}, f32[4,128,128]{2,1,0:T(8,128)S(1)}, s32[]{:T(128)}) %tuple.65), condition=%wide.while_cond.4, body=%wide.while_body.4.sunk | while | flops 2 | bytes 393329 | solution.py:19
  168.8 40.1 %custom-call.30 = f32[4,128,128]{1,2,0:T(8,128)S(1)} custom-call(f32[4,128,128]{2,1,0:T(8,128)} %copy-done.10), custom_call_target="InvertDiagBlocksLowerTriangular" | custom-call | tf_op jit(solution)/shard_map/vmap()/triangular_solve/custom-call.3 | solution.py:19
  213.4 35.5 %all-reduce.10.cloned.1.call-done = f32[1,512,512]{1,2,0:T(8,128)} async-done(((f32[1,512,512]{1,2,0:T(8,128)}), f32[1,512,512]{1,2,0:T(8,128)}) %all-reduce.10.cloned.1.call-update) | async-done | bytes 1048592 | tf_op jit(solution)/shard_map/psum | solution.py:11
  255.4 48.2 %all-reduce.12.cloned.1.call-done = f32[512,512]{0,1:T(8,128)} async-done(((f32[512,512]{0,1:T(8,128)}), f32[512,512]{0,1:T(8,128)}) %all-reduce.12.cloned.1.call-update) | async-done | bytes 1048592 | tf_op jit(solution)/shard_map/psum | solution.py:11
  311.3 50.6 %all-reduce.14.cloned.1.call-done = f32[512,512]{1,0:T(8,128)} async-done(((f32[512,512]{1,0:T(8,128)}), f32[512,512]{1,0:T(8,128)}) %all-reduce.14.cloned.1.call-update) | async-done | bytes 1048592 | tf_op jit(solution)/shard_map/psum | solution.py:11
  367.6 11.7 %cholesky.358 = f32[128,128]{1,0:T(8,128)S(1)} custom-call(f32[128,128]{1,0:T(8,128)S(1)} %cholesky.439), custom_call_target="Cholesky" | custom-call | tf_op jit(solution)/shard_map/jit(cholesky)/cholesky | solution.py:36
  379.5 9.8 %custom-call.31 = f32[1,128,128]{1,2,0:T(8,128)S(1)} custom-call(f32[1,128,128]{2,1,0:T(8,128)S(1)} %get-tuple-element.106), custom_call_target="InvertDiagBlocksLowerTriangular" | custom-call | tf_op jit(solution)/shard_map/jit(cholesky)/cholesky | solution.py:36
  390.0 11.9 %cholesky.377 = f32[128,128]{1,0:T(8,128)S(1)} custom-call(f32[128,128]{1,0:T(8,128)S(1)} %cholesky.443), custom_call_target="Cholesky" | custom-call | tf_op jit(solution)/shard_map/jit(cholesky)/cholesky | solution.py:36
  401.9 9.8 %custom-call.32 = f32[1,128,128]{1,2,0:T(8,128)S(1)} custom-call(f32[1,128,128]{2,1,0:T(8,128)S(1)} %get-tuple-element.103), custom_call_target="InvertDiagBlocksLowerTriangular" | custom-call | tf_op jit(solution)/shard_map/jit(cholesky)/cholesky | solution.py:36
  412.4 11.7 %cholesky.398 = f32[128,128]{1,0:T(8,128)S(1)} custom-call(f32[128,128]{1,0:T(8,128)S(1)} %cholesky.448), custom_call_target="Cholesky" | custom-call | tf_op jit(solution)/shard_map/jit(cholesky)/cholesky | solution.py:36
  424.2 9.8 %custom-call.33 = f32[1,128,128]{1,2,0:T(8,128)S(1)} custom-call(f32[1,128,128]{2,1,0:T(8,128)S(1)} %get-tuple-element.100), custom_call_target="InvertDiagBlocksLowerTriangular" | custom-call | tf_op jit(solution)/shard_map/jit(cholesky)/cholesky | solution.py:36
  434.6 11.9 %cholesky.415 = f32[128,128]{1,0:T(8,128)S(1)} custom-call(f32[128,128]{1,0:T(8,128)S(1)} %convolution_subtract_fusion.11), custom_call_target="Cholesky" | custom-call | tf_op jit(solution)/shard_map/jit(cholesky)/cholesky | solution.py:36
  451.9 8.5 %while.9 = (s32[]{:T(128)}, f32[512,512]{1,0:T(8,128)S(1)}, s32[4,2]{0,1:T(2,128)S(1)}, f32[4,128,128]{2,1,0:T(8,128)S(1)}, s32[]{:T(128)}) while((s32[]{:T(128)}, f32[512,512]{1,0:T(8,128)S(1)}, s32[4,2]{0,1:T(2,128)S(1)}, f32[4,128,128]{2,1,0:T(8,128)S(1)}, s32[]{:T(128)}) %tuple.83), condition=%wide.while_cond.4.clone, body=%wide.while_body.4.clone.sunk | while | flops 2 | bytes 131189 | solution.py:19
  460.4 39.9 %custom-call.34 = f32[4,128,128]{1,2,0:T(8,128)} custom-call(f32[4,128,128]{2,1,0:T(8,128)S(1)} %get-tuple-element.70), custom_call_target="InvertDiagBlocksLowerTriangular" | custom-call | tf_op jit(solution)/shard_map/vmap()/triangular_solve/custom-call.3 | solution.py:19
  509.6 35.6 %all-reduce.16.cloned.1.call-done = f32[1,512,512]{2,1,0:T(8,128)} async-done(((f32[1,512,512]{2,1,0:T(8,128)}), f32[1,512,512]{2,1,0:T(8,128)}) %all-reduce.16.cloned.1.call-update) | async-done | bytes 1048592 | tf_op jit(solution)/shard_map/psum | solution.py:11
  547.5 52.3 %all-reduce.18.cloned.1.call-done = f32[512,512]{1,0:T(8,128)} async-done(((f32[512,512]{1,0:T(8,128)}), f32[512,512]{1,0:T(8,128)}) %all-reduce.18.cloned.1.call-update) | async-done | bytes 1048592 | tf_op jit(solution)/shard_map/psum | solution.py:11
  (160 shorter events, 82.0 us)
Async XLA Ops:
  6.5 58.1 %all-reduce.8.cloned.1.call-start = ((), (), s32[]{:S(2)}) async-start(), calls=%async_computation | async-start | bytes 2097152 | tf_op jit(solution)/shard_map/psum | solution.py:11
  10.0 239.0 %all-reduce.10.cloned.1.call-start = ((), (), s32[]{:S(2)}) async-start(), calls=%async_computation.1 | async-start | bytes 2097152 | tf_op jit(solution)/shard_map/psum | solution.py:11
  64.7 2.6 copy-start.4
  69.3 1.0 copy-start.5
  168.1 0.7 copy-start.10
  213.3 90.3 %all-reduce.12.cloned.1.call-start = ((), (), s32[]{:S(2)}) async-start(), calls=%async_computation.2 | async-start | bytes 2097152 | tf_op jit(solution)/shard_map/psum | solution.py:11
  251.2 1.2 copy-start
  251.3 110.6 %all-reduce.14.cloned.1.call-start = ((), (), s32[]{:S(2)}) async-start(), calls=%async_computation.3 | async-start | bytes 2097152 | tf_op jit(solution)/shard_map/psum | solution.py:11
  253.7 49.9 %copy-start.1 = (f32[512,512]{0,1:T(8,128)S(1)}, f32[512,512]{0,1:T(8,128)}, u32[]{:S(2)}) copy-start(f32[512,512]{0,1:T(8,128)} %fusion.6) | copy-start | bytes 3145732
  310.5 234.7 %all-reduce.16.cloned.1.call-start = ((), (), s32[]{:S(2)}) async-start(), calls=%async_computation.4 | async-start | bytes 2097152 | tf_op jit(solution)/shard_map/psum | solution.py:11
  363.2 1.3 copy-start.3
  366.6 1.0 copy-start.6
  367.6 21.7 %copy-start.7 = (f32[512,512]{1,0:T(8,128)S(1)}, f32[512,512]{1,0:T(8,128)}, u32[]{:S(2)}) copy-start(f32[512,512]{1,0:T(8,128)} %copy-done.6) | copy-start | bytes 3145732
  501.6 0.7 copy-start.8
  506.0 1.0 copy-start.9
  509.6 90.3 %all-reduce.18.cloned.1.call-start = ((), (), s32[]{:S(2)}) async-start(), calls=%async_computation.5 | async-start | bytes 2097152 | tf_op jit(solution)/shard_map/psum | solution.py:11
  547.5 52.4 %copy-start.2 = (f32[1,512,512]{2,1,0:T(8,128)S(1)}, f32[1,512,512]{2,1,0:T(8,128)}, u32[]{:S(2)}) copy-start(f32[1,512,512]{2,1,0:T(8,128)} %all-reduce.16.cloned.1.call-done) | copy-start | bytes 3145732
Sparse Core Ops, SparseCore 0:
  10.1 54.5 all-reduce.7
  213.5 35.4 all-reduce.9
  251.4 52.1 all-reduce.11
  310.7 51.1 all-reduce.13
  509.7 35.4 all-reduce.15
  547.6 52.1 all-reduce.17
where the time goes:
time: 622 us; the launch traced here: 612 us
  waiting for transfers between devices  277 us (45%)
  other arithmetic  254 us (41%)
  local copies, waits for them, and re-layouts  36.9 us (6%)
  matrix products  24.3 us (4%)
  between operations  19.7 us (3%)
    psum x6, waiting for transfers between devices, from_root(): return lax.psum(jnp.where(mine, shard, jnp.zeros_like(shard)), axis)  277 us
    another operation x29, other arithmetic, factor_panel(): factor = jnp.linalg.cholesky(symmetric(diagonal))  158 us
    another operation x5, other arithmetic, right_solve(): lax.linalg.triangular_solve(factor, block, left_side=False, lower=True, t...  80.3 us
    another operation x36, local copies, waits for them, and re-layouts, right_solve(): lax.linalg.triangular_solve(factor, block, left_side=False, lower=True, t...  18.3 us
  transfers between devices with their start and end apart: 6, of which 6 were waited for; matrix products, arithmetic and copies ran while one was open for 1% of the time, Pallas kernels for 0%

commit v1 on v0

v1 whole, which is shorter than its diff:
```python
import functools

import jax
import jax.numpy as jnp
from jax import lax
from jax.experimental import pallas as pl
from jax.experimental.pallas import tpu as pltpu
from jax.sharding import PartitionSpec as P

BLK = 128
G = 8


def nt(a, b):
    return lax.dot_general(
        a, b, (((1,), (1,)), ((), ())),
        precision=lax.Precision.HIGHEST, preferred_element_type=jnp.float32,
    )


def factor_block(a):
    n = BLK
    ng = n // G
    sub = lax.broadcasted_iota(jnp.int32, (G, n), 0)
    lane = lax.broadcasted_iota(jnp.int32, (G, n), 1)
    left = [a[g * G:(g + 1) * G, :] for g in range(ng)]
    right = [jnp.where(lane == sub + g * G, 1.0, 0.0).astype(jnp.float32) for g in range(ng)]
    for g in range(ng):
        own_l, own_r = left[g], right[g]
        lo = g * G
        nxt = g + 1 < ng
        own_c = [jnp.broadcast_to(own_l[:, lo + j:lo + j + 1], (G, n)) for j in range(G)]
        if nxt:
            nx_l, nx_r = left[g + 1], right[g + 1]
            nx_c = [jnp.broadcast_to(nx_l[:, lo + j:lo + j + 1], (G, n)) for j in range(G)]
        rows_l, rows_r = [], []
        for j in range(G):
            q = lax.rsqrt(jnp.broadcast_to(own_c[j][j:j + 1, :], (G, n)))
            row_l = jnp.broadcast_to(own_l[j:j + 1, :], (G, n)) * q
            row_r = jnp.broadcast_to(own_r[j:j + 1, :], (G, n)) * q
            rows_l.append(row_l)
            rows_r.append(row_r)
            mult = own_c[j] * q
            heads = [jnp.broadcast_to(own_c[t][j:j + 1, :], (G, n)) * q for t in range(j + 1, G)]
            for t in range(j + 1, G):
                own_c[t] = own_c[t] - mult * heads[t - j - 1]
            own_l = own_l - mult * row_l
            own_r = own_r - mult * row_r
            if nxt:
                mult = nx_c[j] * q
                for t in range(j + 1, G):
                    nx_c[t] = nx_c[t] - mult * heads[t - j - 1]
                nx_l = nx_l - mult * row_l
                nx_r = nx_r - mult * row_r
        fin_l, fin_r = rows_l[0], rows_r[0]
        for j in range(1, G):
            fin_l = jnp.where(sub == j, rows_l[j], fin_l)
            fin_r = jnp.where(sub == j, rows_r[j], fin_r)
        left[g], right[g] = fin_l, fin_r
        if nxt:
            left[g + 1], right[g + 1] = nx_l, nx_r
        if g + 2 < ng:
            turned = fin_l.T
            for h in range(g + 2, ng):
                tl, tr = left[h], right[h]
                for j in range(G):
                    m = jnp.broadcast_to(turned[h * G:(h + 1) * G, j:j + 1], (G, n))
                    tl = tl - m * rows_l[j]
                    tr = tr - m * rows_r[j]
                left[h], right[h] = tl, tr
    lt = jnp.concatenate(left, 0)
    w = jnp.concatenate(right, 0)
    return lt, w

def kernel(n_r, n_c, n_cc, nb, x_ref, o_ref, work, diag, fbuf, panels,
           f_send, f_recv, p_send, p_recv):
    parts = nb // BLK
    r = lax.axis_index("pr")
    c = lax.axis_index("pc")
    near = lax.rem(c + 1, n_c)

    barrier = pltpu.get_barrier_semaphore()

    def greet(i, _):
        @pl.when(i != r * n_c + c)
        def _():
            pl.semaphore_signal(
                barrier, inc=1, device_id={"pr": i // n_c, "pc": lax.rem(i, n_c)},
                device_id_type=pl.DeviceIdType.MESH)
        return 0

    lax.fori_loop(0, n_r * n_c, greet, 0)
    o_ref[...] = x_ref[...]

    @pl.when(c < 2)
    def _():
        for m in range(parts):
            work[m] = x_ref[0, :, m * BLK:(m + 1) * BLK]

    pl.semaphore_wait(barrier, n_r * n_c - 1)

    def factor_copy(k, m, to):
        ref = fbuf.at[k, m, pl.ds(m * BLK, nb - m * BLK), :]
        return pltpu.make_async_remote_copy(
            src_ref=ref, dst_ref=ref, send_sem=f_send.at[k, m, to], recv_sem=f_recv.at[k, m],
            device_id={"pr": to}, device_id_type=pl.DeviceIdType.MESH)

    def row_copy(k, m, to):
        ref = panels.at[k, 0, m]
        return pltpu.make_async_remote_copy(
            src_ref=ref, dst_ref=ref, send_sem=p_send.at[k, m, to], recv_sem=p_recv.at[k, 0, m],
            device_id={"pc": to}, device_id_type=pl.DeviceIdType.MESH)

    def col_copy(k, m, to):
        slot = 1 + r // n_c
        return pltpu.make_async_remote_copy(
            src_ref=panels.at[k, 0, m], dst_ref=panels.at[k, slot, m],
            send_sem=p_send.at[k, m, n_c + to], recv_sem=p_recv.at[k, slot, m],
            device_id={"pr": to, "pc": lax.rem(r, n_c)}, device_id_type=pl.DeviceIdType.MESH)

    def holds(k, row, col):
        found = (col > k) & (col <= row)
        for b in range(1, n_cc):
            found = found | ((b * n_c + col > k) & (b * n_c + col <= row))
        return found

    def each_row_copy(k, m, act):
        def one(to, _):
            @pl.when((to != k) & holds(k, r, to))
            def _():
                act(row_copy(k, m, to))
            return 0
        lax.fori_loop(0, n_c, one, 0)

    def each_col_copy(k, m, act):
        def one(to, _):
            act(col_copy(k, m, to))
            return 0
        lax.fori_loop(r + 1, n_r, one, 0)

    def each_factor_copy(k, m, act):
        def one(to, _):
            act(factor_copy(k, m, to))
            return 0
        lax.fori_loop(k + 1, n_r, one, 0)

    def step(k, _):
        is_factor = (r == k) & (c == k)
        is_solver = (c == k) & (r > k)

        @pl.when(is_factor)
        def _():
            i0 = lax.broadcasted_iota(jnp.int32, (BLK, BLK), 0)
            i1 = lax.broadcasted_iota(jnp.int32, (BLK, BLK), 1)

            def stage(m, _):
                rows = pl.ds(pl.multiple_of(m * BLK, BLK), BLK)
                low = jnp.where(i0 >= i1, work[m, rows, :], 0.0)
                lt, w = factor_block(jnp.where(i0 >= i1, low, low.T))
                fbuf[k, m, rows, :] = w
                diag[m] = lt
                for mm in range(parts):
                    @pl.when(m == mm)
                    def _():
                        s = (mm + 1) * BLK
                        if s < nb:
                            fbuf[k, mm, s:, :] = nt(work[mm, s:, :], w)
                        each_factor_copy(k, mm, lambda d: d.start())
                        for n in range(mm + 1, parts):
                            t = n * BLK
                            work[n, t:, :] -= nt(fbuf[k, mm, t:, :], fbuf[k, mm, t:t + BLK, :])
                return 0

            lax.fori_loop(0, parts, stage, 0)
            for m in range(parts):
                s, e = m * BLK, (m + 1) * BLK
                if m:
                    o_ref[0, :s, s:e] = jnp.zeros((s, BLK), jnp.float32)
                o_ref[0, s:e, s:e] = jnp.where(i0 <= i1, diag[m], 0.0).T
                if e < nb:
                    o_ref[0, e:, s:e] = fbuf[k, m, e:, :]
            for m in range(parts):
                each_factor_copy(k, m, lambda d: d.wait_send())

        @pl.when(is_solver)
        def _():
            for m in range(parts):
                s, e = m * BLK, (m + 1) * BLK
                factor_copy(k, m, 0).wait_recv()
                part = nt(work[m], fbuf[k, m, s:e, :])
                panels[k, 0, m] = part
                each_row_copy(k, m, lambda d: d.start())
                each_col_copy(k, m, lambda d: d.start())
                o_ref[0, :, s:e] = part
                for n in range(m + 1, parts):
                    work[n] -= nt(part, fbuf[k, m, n * BLK:(n + 1) * BLK, :])

        for m in range(parts):
            @pl.when((c != k) & holds(k, r, c))
            def _():
                row_copy(k, m, near).wait_recv()
            for b in range(n_cc):
                j = b * n_c + c

                @pl.when((j > k) & (j < r))
                def _():
                    pltpu.make_async_remote_copy(
                        src_ref=panels.at[k, 0, m], dst_ref=panels.at[k, 1 + b, m],
                        send_sem=p_send.at[k, m, 0], recv_sem=p_recv.at[k, 1 + b, m],
                        device_id={"pc": near}, device_id_type=pl.DeviceIdType.MESH).wait_recv()

                @pl.when((j > k) & (j <= r))
                def _():
                    slot = jnp.where(j == r, 0, 1 + b)
                    o_ref[b] -= nt(panels[k, 0, m], panels[k, slot, m])

        @pl.when((k == 0) & (c == 1))
        def _():
            for m in range(parts):
                work[m] = o_ref[0, :, m * BLK:(m + 1) * BLK]

        @pl.when(is_solver)
        def _():
            for m in range(parts):
                each_row_copy(k, m, lambda d: d.wait_send())
                each_col_copy(k, m, lambda d: d.wait_send())
        return 0

    lax.fori_loop(0, 2, step, 0)


def on_device(n_r, n_c, matrix):
    _, nb, n_cc, _ = matrix.shape
    parts = nb // BLK
    tiles = jnp.transpose(matrix[0], (1, 0, 2))
    sem = pltpu.SemaphoreType.DMA
    out = pl.pallas_call(
        functools.partial(kernel, n_r, n_c, n_cc, nb),
        out_shape=jax.ShapeDtypeStruct(tiles.shape, jnp.float32),
        in_specs=[pl.BlockSpec(memory_space=pltpu.VMEM)],
        out_specs=pl.BlockSpec(memory_space=pltpu.VMEM),
        scratch_shapes=[
            pltpu.VMEM((parts, nb, BLK), jnp.float32),
            pltpu.VMEM((parts, BLK, BLK), jnp.float32),
            pltpu.VMEM((2, parts, nb, BLK), jnp.float32),
            pltpu.VMEM((2, 1 + n_cc, parts, nb, BLK), jnp.float32),
            sem((2, parts, n_r)),
            sem((2, parts)),
            sem((2, parts, n_c + n_r)),
            sem((2, 1 + n_cc, parts)),
        ],
        compiler_params=pltpu.CompilerParams(
            collective_id=0, has_side_effects=True, vmem_limit_bytes=40 * 2**20),
    )(tiles)
    return jnp.transpose(out, (1, 0, 2))[None]


def solution(mesh):
    n_r, n_c = mesh.shape["pr"], mesh.shape["pc"]
    spec = P("groups", "pr", None, "pc")
    return jax.shard_map(
        functools.partial(on_device, n_r, n_c), mesh=mesh, in_specs=(spec,), out_specs=spec,
        check_vma=False)
```

time: 622 us -> 101 us (0.16)
  the two profiles are of different devices: /device:TPU:0 before, /device:TPU:27 now
where the time goes in v1:
time: 101 us
  Pallas kernels  98 us (97%)
  local copies, waits for them, and re-layouts  3.34 us (3%)
    pallas_call x1, Pallas kernels, on_device(): pl.pallas_call(functools.partial(kernel, n_r, n_c, n_cc, nb), out_shape=j...  98 us
    another operation x1, local copies, waits for them, and re-layouts, on_device(): return jnp.transpose(out, (1, 0, 2))[None]  2.05 us

profile of v1, /device:TPU:27, one launch (start us, length us, event | category | flops | bytes accessed | tf_op | source)
XLA Modules:
  0.0 101.3 jit_solution(15642162303059605088)
XLA Ops:
  0.0 1.3 %copy.5 = f32[1,512,1,512]{3,1,2,0:T(8,128)S(1)} copy(f32[1,512,1,512]{3,2,1,0:T(1,128)} %param.1) | data formatting | bytes 2097152
  1.3 98.0 %shard_map.17 = f32[1,512,512]{2,1,0:T(8,128)S(1)} custom-call(f32[1,512,512]{2,1,0:T(8,128)S(1)} %bitcast.5), custom_call_target="tpu_custom_call" | custom-call | tf_op jit(solution)/shard_map/pallas_call | solution.py:237
  99.3 2.0 %copy.2 = f32[1,512,1,512]{3,2,1,0:T(1,128)} copy(f32[1,512,1,512]{3,1,2,0:T(8,128)S(1)} %bitcast.4) | data formatting | bytes 2097152 | tf_op jit(solution)/shard_map/broadcast_in_dim;transpose | solution.py:255

commit v2 on v1

--- a/solution.py
+++ b/solution.py
@@ -73,7 +73,7 @@
     return lt, w
 
 def kernel(n_r, n_c, n_cc, nb, x_ref, o_ref, work, diag, fbuf, panels,
-           f_send, f_recv, p_send, p_recv):
+           f_send, f_recv, row_send, col_send, p_recv):
     parts = nb // BLK
     r = lax.axis_index("pr")
     c = lax.axis_index("pc")
@@ -92,31 +92,40 @@
     lax.fori_loop(0, n_r * n_c, greet, 0)
     o_ref[...] = x_ref[...]
 
+    i0 = lax.broadcasted_iota(jnp.int32, (BLK, BLK), 0)
+    i1 = lax.broadcasted_iota(jnp.int32, (BLK, BLK), 1)
+
     @pl.when(c < 2)
     def _():
         for m in range(parts):
             work[m] = x_ref[0, :, m * BLK:(m + 1) * BLK]
 
+        @pl.when(r == c)
+        def _():
+            for m in range(parts):
+                block = work[m, m * BLK:(m + 1) * BLK, :]
+                work[m, m * BLK:(m + 1) * BLK, :] = jnp.where(i0 >= i1, block, block.T)
+
     pl.semaphore_wait(barrier, n_r * n_c - 1)
 
-    def factor_copy(k, m, to):
+    def factor_copy(k, m):
         ref = fbuf.at[k, m, pl.ds(m * BLK, nb - m * BLK), :]
         return pltpu.make_async_remote_copy(
-            src_ref=ref, dst_ref=ref, send_sem=f_send.at[k, m, to], recv_sem=f_recv.at[k, m],
-            device_id={"pr": to}, device_id_type=pl.DeviceIdType.MESH)
+            src_ref=ref, dst_ref=ref, send_sem=f_send.at[k, m], recv_sem=f_recv.at[k, m],
+            device_id={"pr": lax.rem(r + 1, n_r)}, device_id_type=pl.DeviceIdType.MESH)
 
     def row_copy(k, m, to):
         ref = panels.at[k, 0, m]
         return pltpu.make_async_remote_copy(
-            src_ref=ref, dst_ref=ref, send_sem=p_send.at[k, m, to], recv_sem=p_recv.at[k, 0, m],
+            src_ref=ref, dst_ref=ref, send_sem=row_send.at[k, m, to], recv_sem=p_recv.at[k, 0, m],
             device_id={"pc": to}, device_id_type=pl.DeviceIdType.MESH)
 
-    def col_copy(k, m, to):
-        slot = 1 + r // n_c
+    def col_copy(k, m, source, slot, to_c):
         return pltpu.make_async_remote_copy(
-            src_ref=panels.at[k, 0, m], dst_ref=panels.at[k, slot, m],
-            send_sem=p_send.at[k, m, n_c + to], recv_sem=p_recv.at[k, slot, m],
-            device_id={"pr": to, "pc": lax.rem(r, n_c)}, device_id_type=pl.DeviceIdType.MESH)
+            src_ref=panels.at[k, source, m], dst_ref=panels.at[k, slot, m],
+            send_sem=col_send.at[k, source, m], recv_sem=p_recv.at[k, slot, m],
+            device_id={"pr": lax.rem(r + 1, n_r), "pc": to_c},
+            device_id_type=pl.DeviceIdType.MESH)
 
     def holds(k, row, col):
         found = (col > k) & (col <= row)
@@ -125,24 +134,36 @@
         return found
 
     def each_row_copy(k, m, act):
-        def one(to, _):
-            @pl.when((to != k) & holds(k, r, to))
+        for to in range(n_c):
+            pair = (k // 2) * 2
+            first = (to == pair + 1 - (k - pair)) | ((to % 2 == 0) & (to != pair))
+
+            @pl.when(first & holds(k, r, to))
             def _():
                 act(row_copy(k, m, to))
-            return 0
-        lax.fori_loop(0, n_c, one, 0)
-
-    def each_col_copy(k, m, act):
-        def one(to, _):
-            act(col_copy(k, m, to))
-            return 0
-        lax.fori_loop(r + 1, n_r, one, 0)
-
-    def each_factor_copy(k, m, act):
-        def one(to, _):
-            act(factor_copy(k, m, to))
-            return 0
-        lax.fori_loop(k + 1, n_r, one, 0)
+
+    def hand_on_row(k, m, act):
+        @pl.when((c % 2 == 0) & (c // 2 != k // 2) & holds(k, r, c + 1))
+        def _():
+            act(row_copy(k, m, lax.rem(c + 1, n_c)))
+
+    def own_col_copy(k, m, act):
+        @pl.when(r + 1 < n_r)
+        def _():
+            act(col_copy(k, m, 0, 1 + r // n_c, lax.rem(r, n_c)))
+
+    def hand_on_col(k, m, b, act):
+        @pl.when(r + 1 < n_r)
+        def _():
+            act(col_copy(k, m, 1 + b, 1 + b, c))
+
+    def hand_on_factor(k, m, act):
+        @pl.when(r + 1 < n_r)
+        def _():
+            act(factor_copy(k, m))
+
+    start = lambda d: d.start()
+    sent = lambda d: d.wait_send()
 
     def step(k, _):
         is_factor = (r == k) & (c == k)
@@ -150,28 +171,25 @@
 
         @pl.when(is_factor)
         def _():
-            i0 = lax.broadcasted_iota(jnp.int32, (BLK, BLK), 0)
-            i1 = lax.broadcasted_iota(jnp.int32, (BLK, BLK), 1)
-
-            def stage(m, _):
-                rows = pl.ds(pl.multiple_of(m * BLK, BLK), BLK)
-                low = jnp.where(i0 >= i1, work[m, rows, :], 0.0)
-                lt, w = factor_block(jnp.where(i0 >= i1, low, low.T))
-                fbuf[k, m, rows, :] = w
+            a = work[0, :BLK, :]
+            for m in range(parts):
+                s, e = m * BLK, (m + 1) * BLK
+                lt, w = factor_block(a)
                 diag[m] = lt
-                for mm in range(parts):
-                    @pl.when(m == mm)
-                    def _():
-                        s = (mm + 1) * BLK
-                        if s < nb:
-                            fbuf[k, mm, s:, :] = nt(work[mm, s:, :], w)
-                        each_factor_copy(k, mm, lambda d: d.start())
-                        for n in range(mm + 1, parts):
-                            t = n * BLK
-                            work[n, t:, :] -= nt(fbuf[k, mm, t:, :], fbuf[k, mm, t:t + BLK, :])
-                return 0
-
-            lax.fori_loop(0, parts, stage, 0)
+                fbuf[k, m, s:e, :] = w
+                if m + 1 < parts:
+                    f = e + BLK
+                    head = nt(work[m, e:f, :], w)
+                    a = work[m + 1, e:f, :] - nt(head, head)
+                    fbuf[k, m, e:f, :] = head
+                    if f < nb:
+                        fbuf[k, m, f:, :] = nt(work[m, f:, :], w)
+                factor_copy(k, m).start()
+                if m + 2 < parts:
+                    work[m + 1, f:, :] -= nt(fbuf[k, m, f:, :], head)
+                for n in range(m + 2, parts):
+                    t = n * BLK
+                    work[n, t:, :] -= nt(fbuf[k, m, t:, :], fbuf[k, m, t:t + BLK, :])
             for m in range(parts):
                 s, e = m * BLK, (m + 1) * BLK
                 if m:
@@ -180,17 +198,18 @@
                 if e < nb:
                     o_ref[0, e:, s:e] = fbuf[k, m, e:, :]
             for m in range(parts):
-                each_factor_copy(k, m, lambda d: d.wait_send())
+                factor_copy(k, m).wait_send()
 
         @pl.when(is_solver)
         def _():
             for m in range(parts):
                 s, e = m * BLK, (m + 1) * BLK
-                factor_copy(k, m, 0).wait_recv()
+                factor_copy(k, m).wait_recv()
+                hand_on_factor(k, m, start)
                 part = nt(work[m], fbuf[k, m, s:e, :])
                 panels[k, 0, m] = part
-                each_row_copy(k, m, lambda d: d.start())
-                each_col_copy(k, m, lambda d: d.start())
+                each_row_copy(k, m, start)
+                own_col_copy(k, m, start)
                 o_ref[0, :, s:e] = part
                 for n in range(m + 1, parts):
                     work[n] -= nt(part, fbuf[k, m, n * BLK:(n + 1) * BLK, :])
@@ -199,31 +218,50 @@
             @pl.when((c != k) & holds(k, r, c))
             def _():
                 row_copy(k, m, near).wait_recv()
+                hand_on_row(k, m, start)
             for b in range(n_cc):
                 j = b * n_c + c
+                active = (j > k) & (j <= r)
+                kept = (k == 0) & (c == 1) if b == 0 else False
 
                 @pl.when((j > k) & (j < r))
                 def _():
-                    pltpu.make_async_remote_copy(
-                        src_ref=panels.at[k, 0, m], dst_ref=panels.at[k, 1 + b, m],
-                        send_sem=p_send.at[k, m, 0], recv_sem=p_recv.at[k, 1 + b, m],
-                        device_id={"pc": near}, device_id_type=pl.DeviceIdType.MESH).wait_recv()
-
-                @pl.when((j > k) & (j <= r))
+                    col_copy(k, m, 1 + b, 1 + b, c).wait_recv()
+                    hand_on_col(k, m, b, start)
+
+                if b == 0:
+                    @pl.when(active & kept & (r == 1))
+                    def _():
+                        for n in range(parts):
+                            t = n * BLK
+                            work[n, t:, :] -= nt(panels[k, 0, m, t:, :], panels[k, 0, m, t:t + BLK, :])
+
+                    @pl.when(active & kept & (r > 1))
+                    def _():
+                        for n in range(parts):
+                            work[n] -= nt(panels[k, 0, m], panels[k, 1, m, n * BLK:(n + 1) * BLK, :])
+
+                @pl.when(active & jnp.logical_not(kept))
                 def _():
                     slot = jnp.where(j == r, 0, 1 + b)
                     o_ref[b] -= nt(panels[k, 0, m], panels[k, slot, m])
 
-        @pl.when((k == 0) & (c == 1))
-        def _():
-            for m in range(parts):
-                work[m] = o_ref[0, :, m * BLK:(m + 1) * BLK]
-
-        @pl.when(is_solver)
-        def _():
-            for m in range(parts):
-                each_row_copy(k, m, lambda d: d.wait_send())
-                each_col_copy(k, m, lambda d: d.wait_send())
+        for m in range(parts):
+            @pl.when(is_solver)
+            def _():
+                hand_on_factor(k, m, sent)
+                each_row_copy(k, m, sent)
+                own_col_copy(k, m, sent)
+
+            @pl.when((c != k) & holds(k, r, c))
+            def _():
+                hand_on_row(k, m, sent)
+            for b in range(n_cc):
+                j = b * n_c + c
+
+                @pl.when((j > k) & (j < r))
+                def _():
+                    hand_on_col(k, m, b, sent)
         return 0
 
     lax.fori_loop(0, 2, step, 0)
@@ -244,9 +282,10 @@
             pltpu.VMEM((parts, BLK, BLK), jnp.float32),
             pltpu.VMEM((2, parts, nb, BLK), jnp.float32),
             pltpu.VMEM((2, 1 + n_cc, parts, nb, BLK), jnp.float32),
-            sem((2, parts, n_r)),
             sem((2, parts)),
-            sem((2, parts, n_c + n_r)),
+            sem((2, parts)),
+            sem((2, parts, n_c)),
+            sem((2, 1 + n_cc, parts)),
             sem((2, 1 + n_cc, parts)),
         ],
         compiler_params=pltpu.CompilerParams(

time: 101 us -> 86.2 us (0.85)
  Pallas kernels: 98 us -> 82.7 us
    pallas_call x1, Pallas kernels: 98 us -> 82.7 us  [on_device(): pl.pallas_call(functools.partial(kernel, n_r, n_c, n_cc, nb), out_shape=j...]
where the time goes in v2:
time: 86.2 us; the launch traced here: 86 us
  Pallas kernels  82.7 us (96%)
  local copies, waits for them, and re-layouts  3.34 us (4%)
    pallas_call x1, Pallas kernels, on_device(): pl.pallas_call(functools.partial(kernel, n_r, n_c, n_cc, nb), out_shape=j...  82.7 us
    another operation x1, local copies, waits for them, and re-layouts, on_device(): return jnp.transpose(out, (1, 0, 2))[None]  2.05 us

profile of v2, /device:TPU:27, one launch (start us, length us, event | category | flops | bytes accessed | tf_op | source)
XLA Modules:
  0.0 86.0 jit_solution(14571757132525187266)
XLA Ops:
  0.0 1.3 %copy.5 = f32[1,512,1,512]{3,1,2,0:T(8,128)S(1)} copy(f32[1,512,1,512]{3,2,1,0:T(1,128)} %param.1) | data formatting | bytes 2097152
  1.3 82.7 %shard_map.17 = f32[1,512,512]{2,1,0:T(8,128)S(1)} custom-call(f32[1,512,512]{2,1,0:T(8,128)S(1)} %bitcast.5), custom_call_target="tpu_custom_call" | custom-call | tf_op jit(solution)/shard_map/pallas_call | solution.py:275
  84.0 2.0 %copy.2 = f32[1,512,1,512]{3,2,1,0:T(1,128)} copy(f32[1,512,1,512]{3,1,2,0:T(8,128)S(1)} %bitcast.4) | data formatting | bytes 2097152 | tf_op jit(solution)/shard_map/broadcast_in_dim;transpose | solution.py:294

commit v3 on v2

--- a/solution.py
+++ b/solution.py
@@ -9,6 +9,7 @@
 
 BLK = 128
 G = 8
+SUPER = 8
 
 
 def nt(a, b):
@@ -25,49 +26,50 @@
     lane = lax.broadcasted_iota(jnp.int32, (G, n), 1)
     left = [a[g * G:(g + 1) * G, :] for g in range(ng)]
     right = [jnp.where(lane == sub + g * G, 1.0, 0.0).astype(jnp.float32) for g in range(ng)]
-    for g in range(ng):
-        own_l, own_r = left[g], right[g]
-        lo = g * G
-        nxt = g + 1 < ng
-        own_c = [jnp.broadcast_to(own_l[:, lo + j:lo + j + 1], (G, n)) for j in range(G)]
-        if nxt:
-            nx_l, nx_r = left[g + 1], right[g + 1]
-            nx_c = [jnp.broadcast_to(nx_l[:, lo + j:lo + j + 1], (G, n)) for j in range(G)]
-        rows_l, rows_r = [], []
-        for j in range(G):
-            q = lax.rsqrt(jnp.broadcast_to(own_c[j][j:j + 1, :], (G, n)))
-            row_l = jnp.broadcast_to(own_l[j:j + 1, :], (G, n)) * q
-            row_r = jnp.broadcast_to(own_r[j:j + 1, :], (G, n)) * q
-            rows_l.append(row_l)
-            rows_r.append(row_r)
-            mult = own_c[j] * q
-            heads = [jnp.broadcast_to(own_c[t][j:j + 1, :], (G, n)) * q for t in range(j + 1, G)]
-            for t in range(j + 1, G):
-                own_c[t] = own_c[t] - mult * heads[t - j - 1]
-            own_l = own_l - mult * row_l
-            own_r = own_r - mult * row_r
-            if nxt:
-                mult = nx_c[j] * q
+    for s0 in range(0, ng, SUPER):
+        s1 = min(s0 + SUPER, ng)
+        for g in range(s0, s1):
+            own_l, own_r = left[g], right[g]
+            lo = g * G
+            later = range(g + 1, s1)
+            own_c = [jnp.broadcast_to(own_l[:, lo + j:lo + j + 1], (G, n)) for j in range(G)]
+            cols = {h: [jnp.broadcast_to(left[h][:, lo + j:lo + j + 1], (G, n)) for j in range(G)]
+                    for h in later}
+            rows_l, rows_r = [], []
+            for j in range(G):
+                q = lax.rsqrt(jnp.broadcast_to(own_c[j][j:j + 1, :], (G, n)))
+                row_l = jnp.broadcast_to(own_l[j:j + 1, :], (G, n)) * q
+                row_r = jnp.broadcast_to(own_r[j:j + 1, :], (G, n)) * q
+                rows_l.append(row_l)
+                rows_r.append(row_r)
+                mult = own_c[j] * q
+                heads = [jnp.broadcast_to(own_c[t][j:j + 1, :], (G, n)) * q for t in range(j + 1, G)]
                 for t in range(j + 1, G):
-                    nx_c[t] = nx_c[t] - mult * heads[t - j - 1]
-                nx_l = nx_l - mult * row_l
-                nx_r = nx_r - mult * row_r
-        fin_l, fin_r = rows_l[0], rows_r[0]
-        for j in range(1, G):
-            fin_l = jnp.where(sub == j, rows_l[j], fin_l)
-            fin_r = jnp.where(sub == j, rows_r[j], fin_r)
-        left[g], right[g] = fin_l, fin_r
-        if nxt:
-            left[g + 1], right[g + 1] = nx_l, nx_r
-        if g + 2 < ng:
-            turned = fin_l.T
-            for h in range(g + 2, ng):
-                tl, tr = left[h], right[h]
-                for j in range(G):
-                    m = jnp.broadcast_to(turned[h * G:(h + 1) * G, j:j + 1], (G, n))
-                    tl = tl - m * rows_l[j]
-                    tr = tr - m * rows_r[j]
-                left[h], right[h] = tl, tr
+                    own_c[t] = own_c[t] - mult * heads[t - j - 1]
+                own_l = own_l - mult * row_l
+                own_r = own_r - mult * row_r
+                for h in later:
+                    c = cols[h]
+                    mult = c[j] * q
+                    for t in range(j + 1, G):
+                        c[t] = c[t] - mult * heads[t - j - 1]
+                    left[h] = left[h] - mult * row_l
+                    right[h] = right[h] - mult * row_r
+            fin_l, fin_r = rows_l[0], rows_r[0]
+            for j in range(1, G):
+                fin_l = jnp.where(sub == j, rows_l[j], fin_l)
+                fin_r = jnp.where(sub == j, rows_r[j], fin_r)
+            left[g], right[g] = fin_l, fin_r
+        if s1 < ng:
+            top = jnp.concatenate(left[s0:s1], 0)
+            both = jnp.concatenate([top, jnp.concatenate(right[s0:s1], 0)], 1)
+            prod = lax.dot_general(top[:, s1 * G:], both, (((0,), (0,)), ((), ())),
+                                   precision=lax.Precision.HIGHEST,
+                                   preferred_element_type=jnp.float32)
+            for h in range(s1, ng):
+                o = (h - s1) * G
+                left[h] = left[h] - prod[o:o + G, :n]
+                right[h] = right[h] - prod[o:o + G, n:]
     lt = jnp.concatenate(left, 0)
     w = jnp.concatenate(right, 0)
     return lt, w
@@ -147,10 +149,10 @@
         def _():
             act(row_copy(k, m, lax.rem(c + 1, n_c)))
 
-    def own_col_copy(k, m, act):
+    def own_col_copy(k, m, b, act):
         @pl.when(r + 1 < n_r)
         def _():
-            act(col_copy(k, m, 0, 1 + r // n_c, lax.rem(r, n_c)))
+            act(col_copy(k, m, 0, 1 + b, c))
 
     def hand_on_col(k, m, b, act):
         @pl.when(r + 1 < n_r)
@@ -209,7 +211,6 @@
                 part = nt(work[m], fbuf[k, m, s:e, :])
                 panels[k, 0, m] = part
                 each_row_copy(k, m, start)
-                own_col_copy(k, m, start)
                 o_ref[0, :, s:e] = part
                 for n in range(m + 1, parts):
                     work[n] -= nt(part, fbuf[k, m, n * BLK:(n + 1) * BLK, :])
@@ -229,6 +230,10 @@
                     col_copy(k, m, 1 + b, 1 + b, c).wait_recv()
                     hand_on_col(k, m, b, start)
 
+                @pl.when((j > k) & (j == r))
+                def _():
+                    own_col_copy(k, m, b, start)
+
                 if b == 0:
                     @pl.when(active & kept & (r == 1))
                     def _():
@@ -251,7 +256,6 @@
             def _():
                 hand_on_factor(k, m, sent)
                 each_row_copy(k, m, sent)
-                own_col_copy(k, m, sent)
 
             @pl.when((c != k) & holds(k, r, c))
             def _():
@@ -262,6 +266,10 @@
                 @pl.when((j > k) & (j < r))
                 def _():
                     hand_on_col(k, m, b, sent)
+
+                @pl.when((j > k) & (j == r))
+                def _():
+                    own_col_copy(k, m, b, sent)
         return 0
 
     lax.fori_loop(0, 2, step, 0)

time: 86.2 us -> 66.6 us (0.77)
  Pallas kernels: 82.7 us -> 62.8 us
    pallas_call x1, Pallas kernels: 82.7 us -> 62.8 us  [on_device(): pl.pallas_call(functools.partial(kernel, n_r, n_c, n_cc, nb), out_shape=j...]
where the time goes in v3:
time: 66.6 us; the launch traced here: 66.2 us
  Pallas kernels  62.8 us (94%)
  local copies, waits for them, and re-layouts  3.34 us (5%)
    pallas_call x1, Pallas kernels, on_device(): pl.pallas_call(functools.partial(kernel, n_r, n_c, n_cc, nb), out_shape=j...  62.8 us
    another operation x1, local copies, waits for them, and re-layouts, on_device(): return jnp.transpose(out, (1, 0, 2))[None]  2.05 us

profile of v3, /device:TPU:27, one launch (start us, length us, event | category | flops | bytes accessed | tf_op | source)
XLA Modules:
  0.0 66.2 jit_solution(3604151605704775312)
XLA Ops:
  0.0 1.3 %copy.5 = f32[1,512,1,512]{3,1,2,0:T(8,128)S(1)} copy(f32[1,512,1,512]{3,2,1,0:T(1,128)} %param.1) | data formatting | bytes 2097152
  1.3 62.8 %shard_map.17 = f32[1,512,512]{2,1,0:T(8,128)S(1)} custom-call(f32[1,512,512]{2,1,0:T(8,128)S(1)} %bitcast.5), custom_call_target="tpu_custom_call" | custom-call | tf_op jit(solution)/shard_map/pallas_call | solution.py:283
  64.1 2.0 %copy.2 = f32[1,512,1,512]{3,2,1,0:T(1,128)} copy(f32[1,512,1,512]{3,1,2,0:T(8,128)S(1)} %bitcast.4) | data formatting | bytes 2097152 | tf_op jit(solution)/shard_map/broadcast_in_dim;transpose | solution.py:302

commit v4 on v3

--- a/solution.py
+++ b/solution.py
@@ -19,7 +19,7 @@
     )
 
 
-def factor_block(a):
+def factor_block(a, jobs=()):
     n = BLK
     ng = n // G
     sub = lax.broadcasted_iota(jnp.int32, (G, n), 0)
@@ -60,6 +60,8 @@
                 fin_l = jnp.where(sub == j, rows_l[j], fin_l)
                 fin_r = jnp.where(sub == j, rows_r[j], fin_r)
             left[g], right[g] = fin_l, fin_r
+            if g < len(jobs):
+                jobs[g]()
         if s1 < ng:
             top = jnp.concatenate(left[s0:s1], 0)
             both = jnp.concatenate([top, jnp.concatenate(right[s0:s1], 0)], 1)
@@ -92,7 +94,14 @@
         return 0
 
     lax.fori_loop(0, n_r * n_c, greet, 0)
-    o_ref[...] = x_ref[...]
+
+    @pl.when((c >= 2) | (r < c))
+    def _():
+        o_ref[0] = x_ref[0]
+
+    for b in range(1, n_cc):
+        o_ref[b] = x_ref[b]
+
 
     i0 = lax.broadcasted_iota(jnp.int32, (BLK, BLK), 0)
     i1 = lax.broadcasted_iota(jnp.int32, (BLK, BLK), 1)
@@ -108,7 +117,9 @@
                 block = work[m, m * BLK:(m + 1) * BLK, :]
                 work[m, m * BLK:(m + 1) * BLK, :] = jnp.where(i0 >= i1, block, block.T)
 
-    pl.semaphore_wait(barrier, n_r * n_c - 1)
+    @pl.when((r != 0) | (c != 0))
+    def _():
+        pl.semaphore_wait(barrier, n_r * n_c - 1)
 
     def factor_copy(k, m):
         ref = fbuf.at[k, m, pl.ds(m * BLK, nb - m * BLK), :]
@@ -174,24 +185,37 @@
         @pl.when(is_factor)
         def _():
             a = work[0, :BLK, :]
+            jobs = []
             for m in range(parts):
                 s, e = m * BLK, (m + 1) * BLK
-                lt, w = factor_block(a)
+                lt, w = factor_block(a, jobs)
                 diag[m] = lt
                 fbuf[k, m, s:e, :] = w
-                if m + 1 < parts:
-                    f = e + BLK
-                    head = nt(work[m, e:f, :], w)
-                    a = work[m + 1, e:f, :] - nt(head, head)
-                    fbuf[k, m, e:f, :] = head
+                if m == 0:
+                    @pl.when(k == 0)
+                    def _():
+                        pl.semaphore_wait(barrier, n_r * n_c - 1)
+                if m + 1 == parts:
+                    factor_copy(k, m).start()
+                    break
+                f = e + BLK
+                head = nt(work[m, e:f, :], w)
+                a = work[m + 1, e:f, :] - nt(head, head)
+                fbuf[k, m, e:f, :] = head
+
+                def finish(m=m, f=f, w=w):
                     if f < nb:
                         fbuf[k, m, f:, :] = nt(work[m, f:, :], w)
-                factor_copy(k, m).start()
-                if m + 2 < parts:
-                    work[m + 1, f:, :] -= nt(fbuf[k, m, f:, :], head)
-                for n in range(m + 2, parts):
-                    t = n * BLK
-                    work[n, t:, :] -= nt(fbuf[k, m, t:, :], fbuf[k, m, t:t + BLK, :])
+                    factor_copy(k, m).start()
+
+                def trail(n, m=m, e=e):
+                    t = max(n * BLK, e + BLK)
+                    work[n, t:, :] -= nt(fbuf[k, m, t:, :], fbuf[k, m, n * BLK:(n + 1) * BLK, :])
+
+                jobs = [finish]
+                for n in range(m + 1, parts):
+                    if max(n * BLK, f) < nb:
+                        jobs.append(functools.partial(trail, n))
             for m in range(parts):
                 s, e = m * BLK, (m + 1) * BLK
                 if m:

time: 66.6 us -> 62.8 us (0.943)
  Pallas kernels: 62.8 us -> 59.1 us
    pallas_call x1, Pallas kernels: 62.8 us -> 59.1 us  [on_device(): pl.pallas_call(functools.partial(kernel, n_r, n_c, n_cc, nb), out_shape=j...]
where the time goes in v4:
time: 62.8 us; the launch traced here: 62.5 us
  Pallas kernels  59.1 us (94%)
  local copies, waits for them, and re-layouts  3.34 us (5%)
    pallas_call x1, Pallas kernels, on_device(): pl.pallas_call(functools.partial(kernel, n_r, n_c, n_cc, nb), out_shape=j...  59.1 us
    another operation x1, local copies, waits for them, and re-layouts, on_device(): return jnp.transpose(out, (1, 0, 2))[None]  2.05 us
    unnamed x1, local copies, waits for them, and re-layouts  1.29 us

profile of v4, /device:TPU:27, one launch (start us, length us, event | category | flops | bytes accessed | tf_op | source)
XLA Modules:
  0.0 62.5 jit_solution(4471070600163379091)
XLA Ops:
  0.0 1.3 %copy.5 = f32[1,512,1,512]{3,1,2,0:T(8,128)S(1)} copy(f32[1,512,1,512]{3,2,1,0:T(1,128)} %param.1) | data formatting | bytes 2097152
  1.3 59.1 %shard_map.17 = f32[1,512,512]{2,1,0:T(8,128)S(1)} custom-call(f32[1,512,512]{2,1,0:T(8,128)S(1)} %bitcast.5), custom_call_target="tpu_custom_call" | custom-call | tf_op jit(solution)/shard_map/pallas_call | solution.py:307
  60.4 2.0 %copy.2 = f32[1,512,1,512]{3,2,1,0:T(1,128)} copy(f32[1,512,1,512]{3,1,2,0:T(8,128)S(1)} %bitcast.4) | data formatting | bytes 2097152 | tf_op jit(solution)/shard_map/broadcast_in_dim;transpose | solution.py:326
